TPU v7x, 32 devices: a whole 2x2x4 slice. The times are simulated.
32 devices in a mesh: groups: 2 (over y), expert: 16 (over z, x, core).
Axes of the slice: x: 2, y: 2, z: 4, core: 2. Of those that a mesh axis runs over, the one named last changes fastest.
Arguments:
- tokens: bfloat16 [2048, 2048], P(('groups', 'expert')), parts along dimension 0, may hold values from -6 to 6
- expert_ids: int32 [2048, 8], P(('groups', 'expert')), parts along dimension 0, may hold values from 0 to 15, all different within a row; in each aligned block of 64 rows (0 to 63, 64 to 127, ...) at most 48 rows name the same one
- gate_scores: float32 [2048, 8], P(('groups', 'expert')), parts along dimension 0, may hold values from 0.05 to 1
- host_expert: int32 [16], replicated, may hold values from 0 to 15, each once
- w_in: bfloat16 [16, 2048, 1536], P('expert'), may hold values from -0.125 to 0.125
- w_down: bfloat16 [16, 768, 2048], P('expert'), may hold values from -0.625 to 0.625
Outputs:
- mixed: bfloat16 [2048, 2048], P(('groups', 'expert')), parts along dimension 0
There are 2 independent parts, one for each index of `groups`. A program takes and returns all parts, laid end to end along the dimension named above; an argument that names none is the same for every part. Nothing has to cross between parts.
Inputs may be any that keep to these rules, and one draw needn't show every extreme that they name: `expert_ids`: each token names 8 different experts; the tokens of one device name no expert more than 48 times, a bound that some block reaches. `host_expert`: each expert stands in exactly one slot.
All inputs are finite; a program needn't handle non-finite values.
Results may differ from a plain program's by a relative error of at most 0.0057.
Values may be sent and summed in bfloat16 or wider, within the bound.
A program may use at most 64 MiB of HBM per device.

v0:
```python
import jax
import jax.numpy as jnp
from jax import lax
from jax.sharding import PartitionSpec as P


def expert_block(rows_in, gate_up, down_proj, hidden_width):
    pair = jnp.dot(rows_in, gate_up, preferred_element_type=jnp.float32)
    active = (jax.nn.silu(pair[:, :hidden_width]) * pair[:, hidden_width:]).astype(jnp.bfloat16)
    return jnp.dot(active, down_proj, preferred_element_type=jnp.float32).astype(jnp.bfloat16)


def shards(tokens, expert_ids, gate_scores, host_expert, w_in, w_down):
    tok_rows, width_model = tokens.shape
    top_count = expert_ids.shape[1]
    hosts = lax.axis_size("expert")
    experts = host_expert.shape[0]
    capacity = 3 * tok_rows * top_count // (2 * experts)
    hidden_width = w_down.shape[1]
    routed = tok_rows * top_count
    slots = hosts * capacity
    gate_up = w_in[0]
    down_proj = w_down[0]
    expert_range = jnp.arange(experts, dtype=jnp.int32)
    host_range = jnp.arange(hosts, dtype=jnp.int32)
    placed = (host_expert[:, None] == expert_range[None, :]).astype(jnp.int32)
    host_of = jnp.sum(placed * host_range[:, None], axis=0)
    flat_ids = expert_ids.reshape(-1)
    id_match = flat_ids[:, None] == expert_range[None, :]
    dest_host = jnp.sum(jnp.where(id_match, host_of[None, :], 0), axis=1)
    row_token = jnp.arange(routed, dtype=jnp.int32) // top_count
    padded_tokens = jnp.concatenate([tokens, jnp.zeros((1, width_model), tokens.dtype)], axis=0)
    earlier = (
        lax.broadcasted_iota(jnp.int32, (routed, routed), 0)
        > lax.broadcasted_iota(jnp.int32, (routed, routed), 1)
    ).astype(jnp.bfloat16)
    dest_match = dest_host[:, None] == host_range[None, :]
    before = jnp.dot(earlier, dest_match.astype(jnp.bfloat16), preferred_element_type=jnp.float32)
    position = jnp.sum(jnp.where(dest_match, before, 0.0), axis=1).astype(jnp.int32)
    slot_of_row = dest_host * capacity + position
    source_row = jnp.full((slots + 1,), tok_rows, jnp.int32).at[slot_of_row].set(row_token)[:slots]
    outgoing = padded_tokens[source_row].reshape(hosts, capacity, width_model)
    received = lax.all_to_all(outgoing, "expert", split_axis=0, concat_axis=0, tiled=True)
    flat_in = received.reshape(-1, width_model)
    served = expert_block(flat_in, gate_up, down_proj, hidden_width).reshape(received.shape)
    returned = lax.all_to_all(served, "expert", split_axis=0, concat_axis=0, tiled=True)
    expert_rows = returned.reshape(slots, width_model)[slot_of_row]
    weights = gate_scores / jnp.sum(gate_scores, axis=1, keepdims=True)
    mixed = jnp.sum(
        weights[:, :, None]
        * expert_rows.reshape(tok_rows, top_count, width_model).astype(jnp.float32),
        axis=1,
    )
    return mixed.astype(jnp.bfloat16)


def solution(mesh):
    placed = (
        P(("groups", "expert"), None),
        P(("groups", "expert"), None),
        P(("groups", "expert"), None),
        P(),
        P("expert", None, None),
        P("expert", None, None),
    )
    return jax.shard_map(
        shards, mesh=mesh, in_specs=placed, out_specs=P(("groups", "expert"), None), check_vma=False
    )
```

profile of v0, /device:TPU:15, one launch (start us, length us, event | category | flops | bytes accessed | tf_op | source)
XLA Modules:
  0.0 184.5 jit_solution(10069609783765678601)
XLA Ops:
  0.0 0.0 copy-start
  0.0 0.9 copy.11
  0.9 0.1 eq.20
  1.0 0.7 select_reduce_fusion.1
  1.8 0.1 select_reduce_fusion
  1.9 0.3 fusion.7
  2.2 2.4 %scatter_custom_fusion = s32[769]{0:T(1024)S(1)} fusion(s32[512]{0:T(512)S(1)} %bitcast.22, s32[512]{0:T(512)S(1)} %add_select_fusion, s32[]{:T(128)} %constant.28.clone.1), kind=kCustom, calls=%fused_computation.33 | custom fusion | bytes 3080 | tf_op jit(solution)/shard_map/scatter | solution.py:41
  4.6 1.0 concatenate.3
  5.6 4.3 %gather_fusion = bf16[768,2048]{1,0:T(8,128)(2,1)} fusion(bf16[65,2048]{1,0:T(8,128)(2,1)S(1)} %concatenate.3, s32[1024]{0:T(1024)S(1)} %pad_clamp_fusion.1), kind=kCustom, calls=%fused_computation | custom fusion | bytes 6294528 | tf_op jit(solution)/shard_map/gather | solution.py:42
  9.9 76.3 %all_to_all.10 = bf16[16,48,2048]{2,1,0:T(8,128)(2,1)S(1)} all-to-all(bf16[16,48,2048]{2,1,0:T(8,128)(2,1)} %bitcast.17), channel_id=1, replica_groups=mesh['groups'=2,'expert'=16] {'expert'}, dimensions={0} | all-to-all | bytes 6291456 | tf_op jit(solution)/shard_map/all_to_all | solution.py:43
  86.2 7.1 %fusion = f32[768,1536]{1,0:T(8,128)S(1)} fusion(bf16[768,2048]{1,0:T(8,128)(2,1)S(1)} %bitcast.19, bf16[1,2048,1536]{2,1,0:T(8,128)(2,1)} %param.10), kind=kOutput, calls=%fused_computation.3 | convolution fusion | flops 4831838208 | bytes 14155776 | tf_op jit(solution)/shard_map/dot_general | solution.py:8
  93.4 0.0 copy-done
  93.4 4.1 %convolution_convert_fusion = bf16[768,2048]{1,0:T(8,128)(2,1)} fusion(bf16[1,768,2048]{2,1,0:T(8,128)(2,1)S(1)} %copy-done, f32[768,1536]{1,0:T(8,128)S(1)} %fusion), kind=kOutput, calls=%fused_computation.7 | convolution fusion | flops 2421030912 | bytes 11010048 | tf_op jit(solution)/shard_map/dot_general | solution.py:10
  97.5 0.0 copy-start.1
  97.5 5.3 %all-to-all-start.1 = ((bf16[16,48,2048]{2,1,0:T(8,128)(2,1)}), bf16[16,48,2048]{2,1,0:T(8,128)(2,1)}, u32[]{:S(2)}, u32[]{:S(2)}) async-start(bf16[16,48,2048]{2,1,0:T(8,128)(2,1)} %bitcast.18), calls=%async_computation.1 | async-start | bytes 6291456 | tf_op jit(solution)/shard_map/all_to_all | solution.py:46
  102.8 0.0 copy-done.1
  102.9 0.1 copy.10
  103.0 69.9 %all-to-all-done.1 = bf16[16,48,2048]{2,1,0:T(8,128)(2,1)} async-done(((bf16[16,48,2048]{2,1,0:T(8,128)(2,1)}), bf16[16,48,2048]{2,1,0:T(8,128)(2,1)}, u32[]{:S(2)}, u32[]{:S(2)}) %all-to-all-start.1) | async-done | bytes 3145760 | tf_op jit(solution)/shard_map/all_to_all | solution.py:46
  172.8 7.5 %gather_fusion.1 = bf16[512,2048]{1,0:T(8,128)(2,1)} fusion(bf16[768,2048]{1,0:T(8,128)(2,1)} %bitcast.7, s32[1024]{0:T(1024)S(1)} %pad_clamp_fusion), kind=kCustom, calls=%fused_computation.1 | custom fusion | bytes 4196352 | tf_op jit(solution)/shard_map/gather | solution.py:47
  180.3 4.1 %fusion.2 = bf16[64,2048]{1,0:T(8,128)(2,1)} fusion(bf16[512,2048]{1,0:T(8,128)(2,1)} %gather_fusion.1, f32[64,8]{1,0:T(8,128)S(1)} %copy.10), kind=kLoop, calls=%fused_computation.6 | loop fusion | flops 3014656 | bytes 2361344 | tf_op jit(solution)/shard_map/reduce_sum | solution.py:49
  (8 shorter events, 0.1 us)
Async XLA Ops:
  0.0 93.4 %copy-start = (bf16[1,768,2048]{2,1,0:T(8,128)(2,1)S(1)}, bf16[1,768,2048]{2,1,0:T(8,128)(2,1)}, u32[]{:S(2)}) copy-start(bf16[1,768,2048]{2,1,0:T(8,128)(2,1)} %param.11) | copy-start | bytes 9437188
  97.5 5.3 %copy-start.1 = (f32[64,8]{0,1:T(8,128)S(1)}, f32[64,8]{0,1:T(8,128)}, u32[]{:S(2)}) copy-start(f32[64,8]{0,1:T(8,128)} %param.8) | copy-start | bytes 6148
  97.5 75.3 %all-to-all-start.1 = ((bf16[16,48,2048]{2,1,0:T(8,128)(2,1)}), bf16[16,48,2048]{2,1,0:T(8,128)(2,1)}, u32[]{:S(2)}, u32[]{:S(2)}) async-start(bf16[16,48,2048]{2,1,0:T(8,128)(2,1)} %bitcast.18), calls=%async_computation.1 | async-start | bytes 6291456 | tf_op jit(solution)/shard_map/all_to_all | solution.py:46
where the time goes:
time: 185 us; the launch traced here: 184 us
  blocking collectives  76.3 us (41%)
  waiting for transfers between devices  69.9 us (38%)
  local copies, waits for them, and re-layouts  16.3 us (9%)
  matrix products  11.5 us (6%)
  starting transfers between devices  5.33 us (3%)
  other arithmetic  5.03 us (3%)
    all_to_all x1, blocking collectives, shards(): lax.all_to_all(outgoing, 'expert', split_axis=0, concat_axis=0, tiled=True)  76.3 us
    all_to_all x1, waiting for transfers between devices, shards(): lax.all_to_all(served, 'expert', split_axis=0, concat_axis=0, tiled=True)  69.9 us
    gather x1, local copies, waits for them, and re-layouts, shards(): expert_rows = returned.reshape(slots, width_model)[slot_of_row]  7.52 us
    dot_general x1, matrix products, expert_block(): pair = jnp.dot(rows_in, gate_up, preferred_element_type=jnp.float32)  7.14 us
    all_to_all x1, starting transfers between devices, shards(): lax.all_to_all(served, 'expert', split_axis=0, concat_axis=0, tiled=True)  5.33 us
    gather x1, local copies, waits for them, and re-layouts, shards(): outgoing = padded_tokens[source_row].reshape(hosts, capacity, width_model)  4.27 us
    reduce_sum x1, other arithmetic, shards(): jnp.sum(weights[:, :, None] * expert_rows.reshape(tok_rows, top_count, wi...  4.14 us
    dot_general x1, matrix products, expert_block(): jnp.dot(active, down_proj, preferred_element_type=jnp.float32)  4.13 us
  transfers between devices with their start and end apart: 1, of which 1 were waited for; matrix products, arithmetic and copies ran while one was open for 0% of the time, Pallas kernels for 0%

commit v1 on v0

--- a/solution.py
+++ b/solution.py
@@ -1,6 +1,8 @@
 import jax
 import jax.numpy as jnp
 from jax import lax
+from jax.experimental import pallas as pl
+from jax.experimental.pallas import tpu as pltpu
 from jax.sharding import PartitionSpec as P
 
 
@@ -10,7 +12,7 @@
     return jnp.dot(active, down_proj, preferred_element_type=jnp.float32).astype(jnp.bfloat16)
 
 
-def shards(tokens, expert_ids, gate_scores, host_expert, w_in, w_down):
+def routed_shards(tokens, expert_ids, gate_scores, host_expert, w_in, w_down):
     tok_rows, width_model = tokens.shape
     top_count = expert_ids.shape[1]
     hosts = lax.axis_size("expert")
@@ -54,7 +56,226 @@
     return mixed.astype(jnp.bfloat16)
 
 
+ORDER = (1, 3, 2, 0)
+SIDE = 128
+TILE = 256
+
+
+def fused_kernel(
+    tok_ref, ids_ref, gate_ref, host_ref, win_ref, wdn_ref, out_ref,
+    xbuf, win, wdn, act, tile_out, part, sib_out, sib_in, x_out, x_in, z_out, z_in, own,
+    load_sem, ag_recv, ag_z, ag_x, ag_s, rs_s, rs_s_in, rs_x, rs_x_in, rs_z, rs_z_in,
+):
+    rows, width = tok_ref.shape
+    experts = host_ref.shape[0]
+    top = ids_ref.shape[1]
+    hidden = wdn_ref.shape[0]
+    group = 4 * rows
+    me = lax.axis_index("expert")
+    z = me // 4
+    x = (me // 2) % 2
+    c = me % 2
+    nbr_x = me + 2 - 4 * x
+    sib = me + 1 - 2 * c
+
+    def far(k):
+        return z + (k % 2) * (1 - 2 * (z % 2)) + (k // 2) * 2 * (1 - 2 * (z // 2))
+
+    load_tok = pltpu.make_async_copy(
+        tok_ref, xbuf.at[pl.ds(pl.multiple_of(me * rows, rows), rows), pl.ds(0, width)], load_sem.at[0])
+    load_tok.start()
+    load_in = pltpu.make_async_copy(win_ref, win, load_sem.at[1])
+    load_in.start()
+    load_dn = pltpu.make_async_copy(wdn_ref, wdn, load_sem.at[2])
+    load_dn.start()
+
+    barrier = pltpu.get_barrier_semaphore()
+    peers = [far(k) * 4 + x * 2 + c for k in range(1, 4)] + [nbr_x, sib]
+    for peer in peers:
+        pl.semaphore_signal(barrier, inc=1, device_id={"expert": peer}, device_id_type=pl.DeviceIdType.MESH)
+
+    lane = lax.broadcasted_iota(jnp.int32, (rows, SIDE), 1)
+    held = jnp.full((rows, SIDE), -1, jnp.int32)
+    for h in range(experts):
+        held = jnp.where((lane == h) | (lane == h + experts), host_ref[h], held)
+    gate = gate_ref[...]
+    weights = gate / jnp.sum(gate, axis=1, keepdims=True)
+    ids = ids_ref[...]
+    dense = jnp.zeros((rows, SIDE), jnp.float32)
+    for k in range(top):
+        dense = dense + jnp.where(ids[:, k:k + 1] == held, weights[:, k:k + 1], 0.0)
+    high = dense.astype(jnp.bfloat16).astype(jnp.float32)
+    coded = jnp.where(lane < experts, high, dense - high).astype(jnp.bfloat16)
+    xbuf[pl.ds(pl.multiple_of(me * rows, rows), rows), pl.ds(width, SIDE)] = coded
+
+    load_tok.wait()
+    pl.semaphore_wait(barrier, len(peers))
+
+    def ag(block, send_sem, target):
+        place = xbuf.at[pl.ds(pl.multiple_of(block * rows, rows), rows)]
+        return pltpu.make_async_remote_copy(
+            src_ref=place, dst_ref=place, send_sem=send_sem, recv_sem=ag_recv.at[block],
+            device_id={"expert": target}, device_id_type=pl.DeviceIdType.MESH)
+
+    def arrived(block):
+        ag(block, ag_s.at[0], sib).wait_recv()
+
+    sends = []
+
+    def start(copy):
+        copy.start()
+        sends.append(copy)
+
+    def mine(k):
+        return far(k) * 4 + x * 2 + c
+
+    def across(k):
+        return far(k) * 4 + (1 - x) * 2 + c
+
+    for k in [k for k in ORDER if k]:
+        start(ag(me, ag_z.at[k], far(k) * 4 + x * 2 + c))
+    start(ag(me, ag_x.at[0], nbr_x))
+    start(ag(me, ag_s.at[0], sib))
+
+    def take_z(k):
+        if k:
+            arrived(mine(k))
+            start(ag(mine(k), ag_x.at[k], nbr_x))
+            start(ag(mine(k), ag_s.at[k], sib))
+
+    def take_x(k):
+        arrived(across(k))
+        start(ag(across(k), ag_s.at[4 + k], sib))
+
+    def take_s(k):
+        arrived(far(k) * 4 + x * 2 + 1 - c)
+        arrived(far(k) * 4 + (1 - x) * 2 + 1 - c)
+
+    def up(k):
+        base = pl.multiple_of(far(k) * group, group)
+
+        @pl.loop(0, hidden // TILE)
+        def _(j):
+            at = pl.multiple_of(j * TILE, TILE)
+            rows_in = xbuf[pl.ds(base, group), pl.ds(0, width)]
+            g = jnp.dot(rows_in, win[:, pl.ds(at, TILE)], preferred_element_type=jnp.float32)
+            u = jnp.dot(rows_in, win[:, pl.ds(hidden + at, TILE)], preferred_element_type=jnp.float32)
+            act[:, pl.ds(at, TILE)] = (jax.nn.silu(g) * u).astype(jnp.bfloat16)
+
+    def down(k):
+        base = pl.multiple_of(far(k) * group, group)
+        side = xbuf[pl.ds(base, group), pl.ds(width, SIDE)].astype(jnp.float32)
+        spot = lax.broadcasted_iota(jnp.int32, (group, SIDE), 1)
+        scale = jnp.sum(jnp.where((spot == me) | (spot == me + experts), side, 0.0), axis=1, keepdims=True)
+
+        @pl.loop(0, width // TILE)
+        def _(n):
+            at = pl.multiple_of(n * TILE, TILE)
+            o = jnp.dot(act[...], wdn[:, pl.ds(at, TILE)], preferred_element_type=jnp.float32)
+            tile_out[...] = o.astype(jnp.bfloat16).astype(jnp.float32) * scale
+            for i in range(2):
+                there = pl.multiple_of((i * 2 + 1 - c) * rows, rows)
+                here = pl.multiple_of((i * 2 + c) * rows, rows)
+                sib_out[k, pl.ds(i * rows, rows), pl.ds(at, TILE)] = tile_out[pl.ds(there, rows), :].astype(jnp.bfloat16)
+                part[k, pl.ds(i * rows, rows), pl.ds(at, TILE)] = tile_out[pl.ds(here, rows), :]
+
+    def remote(src, dst, send_sem, recv_sem, target):
+        return pltpu.make_async_remote_copy(
+            src_ref=src, dst_ref=dst, send_sem=send_sem, recv_sem=recv_sem,
+            device_id={"expert": target}, device_id_type=pl.DeviceIdType.MESH)
+
+    def sib_copy(k):
+        return remote(sib_out.at[k], sib_in.at[k], rs_s.at[k], rs_s_in.at[k], sib)
+
+    def x_copy(k):
+        return remote(x_out.at[k], x_in.at[k], rs_x.at[k], rs_x_in.at[k], nbr_x)
+
+    def z_copy(k):
+        return remote(z_out.at[k], z_in.at[k], rs_z.at[k], rs_z_in.at[k], far(k) * 4 + x * 2 + c)
+
+    def fold_sib(k):
+        sib_copy(k).wait_recv()
+        other = pl.ds(pl.multiple_of((1 - x) * rows, rows), rows)
+        x_out[k] = (part[k, other, :] + sib_in[k, other, :].astype(jnp.float32)).astype(jnp.bfloat16)
+        start(x_copy(k))
+
+    def fold_x(k):
+        x_copy(k).wait_recv()
+        keep = pl.ds(pl.multiple_of(x * rows, rows), rows)
+        total = part[k, keep, :] + sib_in[k, keep, :].astype(jnp.float32) + x_in[k].astype(jnp.float32)
+        if k:
+            z_out[k] = total.astype(jnp.bfloat16)
+            start(z_copy(k))
+        else:
+            own[...] = total
+
+    take_z(ORDER[0])
+    for i, k in enumerate(ORDER):
+        take_x(k)
+        take_s(k)
+        if i == 0:
+            load_in.wait()
+        up(k)
+        if i + 1 < len(ORDER):
+            take_z(ORDER[i + 1])
+        if i:
+            fold_sib(ORDER[i - 1])
+        else:
+            load_dn.wait()
+        down(k)
+        start(sib_copy(k))
+        if i:
+            fold_x(ORDER[i - 1])
+    fold_sib(ORDER[-1])
+    fold_x(ORDER[-1])
+    for k in range(1, 4):
+        z_copy(k).wait_recv()
+    out_ref[...] = (
+        own[...] + z_in[1].astype(jnp.float32) + z_in[2].astype(jnp.float32) + z_in[3].astype(jnp.float32)
+    ).astype(jnp.bfloat16)
+    for copy in sends:
+        copy.wait_send()
+
+
+def gathered_shards(tokens, expert_ids, gate_scores, host_expert, w_in, w_down):
+    rows, width = tokens.shape
+    hosts = lax.axis_size("expert")
+    hidden = w_down.shape[1]
+    vmem = pl.BlockSpec(memory_space=pltpu.VMEM)
+    any_space = pl.BlockSpec(memory_space=pl.ANY)
+    bf16, f32 = jnp.bfloat16, jnp.float32
+    dma = pltpu.SemaphoreType.DMA
+    return pl.pallas_call(
+        fused_kernel,
+        out_shape=jax.ShapeDtypeStruct((rows, width), bf16),
+        in_specs=[any_space, vmem, vmem, pl.BlockSpec(memory_space=pltpu.SMEM), any_space, any_space],
+        out_specs=vmem,
+        scratch_shapes=[
+            pltpu.VMEM((hosts * rows, width + SIDE), bf16),
+            pltpu.VMEM((width, 2 * hidden), bf16),
+            pltpu.VMEM((hidden, width), bf16),
+            pltpu.VMEM((4 * rows, hidden), bf16),
+            pltpu.VMEM((4 * rows, TILE), f32),
+            pltpu.VMEM((4, 2 * rows, width), f32),
+            pltpu.VMEM((4, 2 * rows, width), bf16),
+            pltpu.VMEM((4, 2 * rows, width), bf16),
+            pltpu.VMEM((4, rows, width), bf16),
+            pltpu.VMEM((4, rows, width), bf16),
+            pltpu.VMEM((4, rows, width), bf16),
+            pltpu.VMEM((4, rows, width), bf16),
+            pltpu.VMEM((rows, width), f32),
+            dma((3,)), dma((hosts,)), dma((4,)), dma((4,)), dma((8,)),
+            dma((4,)), dma((4,)), dma((4,)), dma((4,)), dma((4,)), dma((4,)),
+        ],
+        compiler_params=pltpu.CompilerParams(
+            collective_id=0, has_side_effects=True, vmem_limit_bytes=48 * 1024 * 1024),
+        cost_estimate=pl.CostEstimate(
+            flops=6 * hosts * rows * width * hidden, bytes_accessed=6 * width * hidden, transcendentals=0),
+    )(tokens, expert_ids, gate_scores, host_expert, w_in[0], w_down[0])
+
+
 def solution(mesh):
+    shards = gathered_shards if mesh.shape["expert"] == 16 else routed_shards
     placed = (
         P(("groups", "expert"), None),
         P(("groups", "expert"), None),

time: 185 us -> 89.6 us (0.48)
  the two profiles are of different devices: /device:TPU:15 before, /device:TPU:0 now
where the time goes in v1:
time: 89.6 us; the launch traced here: 89.4 us
  Pallas kernels  83.6 us (93%)
  local copies, waits for them, and re-layouts  5.74 us (6%)
    pallas_call x1, Pallas kernels, gathered_shards(): pl.pallas_call(fused_kernel, out_shape=jax.ShapeDtypeStruct((rows, width)...  83.6 us
    unnamed x9, local copies, waits for them, and re-layouts  5.74 us

profile of v1, /device:TPU:0, one launch (start us, length us, event | category | flops | bytes accessed | tf_op | source)
XLA Modules:
  0.0 89.4 jit_solution(1873408571305811752)
XLA Ops:
  0.0 0.8 copy.7.ids_ref
  0.8 0.8 copy.8.gate_ref
  1.5 0.0 copy-start
  1.5 1.9 %copy-done = bf16[1,768,2048]{2,1,0:T(8,128)(2,1)S(1)} copy-done((bf16[1,768,2048]{2,1,0:T(8,128)(2,1)S(1)}, bf16[1,768,2048]{2,1,0:T(8,128)(2,1)}, u32[]{:S(2)}) %copy-start) | copy-done | bytes 3145752
  3.4 0.0 copy-start.1
  3.4 0.9 %copy-done.1 = bf16[64,2048]{1,0:T(8,128)(2,1)S(1)} copy-done((bf16[64,2048]{1,0:T(8,128)(2,1)S(1)}, bf16[64,2048]{1,0:T(8,128)(2,1)}, u32[]{:S(2)}) %copy-start.1) | copy-done | bytes 262168
  4.4 0.0 copy-start.2
  4.4 0.7 copy-done.2
  5.0 83.6 %shard_map.64 = bf16[64,2048]{1,0:T(8,128)(2,1)S(1)} custom-call(bf16[64,2048]{1,0:T(8,128)(2,1)S(1)} %copy-done.1, s32[64,8]{1,0:T(8,128)S(1)} %copy.7.ids_ref, f32[64,8]{1,0:T(8,128)S(1)} %copy.8.gate_ref, s32[16]{0:T(128)S(1)} %copy-done.2, bf16[2048,1536]{1,0:T(8,128)(2,1)} %bitcast.3, bf16[768,2048]{1,0:T(8,128)(2,1)S(1)} %bitcast.2), custom_call_target="tpu_custom_call" | custom-call | flops 9663676416 | bytes 9437184 | tf_op jit(solution)/shard_map/pallas_call | solution.py:248
  88.7 0.7 copy.10
Async XLA Ops:
  1.5 1.9 %copy-start = (bf16[1,768,2048]{2,1,0:T(8,128)(2,1)S(1)}, bf16[1,768,2048]{2,1,0:T(8,128)(2,1)}, u32[]{:S(2)}) copy-start(bf16[1,768,2048]{2,1,0:T(8,128)(2,1)} %param.11) | copy-start | bytes 9437188
  3.4 0.9 %copy-start.1 = (bf16[64,2048]{1,0:T(8,128)(2,1)S(1)}, bf16[64,2048]{1,0:T(8,128)(2,1)}, u32[]{:S(2)}) copy-start(bf16[64,2048]{1,0:T(8,128)(2,1)} %tok_ref.1) | copy-start | bytes 786436
  4.4 0.7 copy-start.2

commit v2 on v1

--- a/solution.py
+++ b/solution.py
@@ -56,7 +56,7 @@
     return mixed.astype(jnp.bfloat16)
 
 
-ORDER = (1, 3, 2, 0)
+ORDER = (3, 1, 2, 0)
 SIDE = 128
 TILE = 256
 
@@ -211,21 +211,21 @@
 
     take_z(ORDER[0])
     for i, k in enumerate(ORDER):
+        if i:
+            fold_sib(ORDER[i - 1])
+        if i + 1 < len(ORDER):
+            take_z(ORDER[i + 1])
         take_x(k)
         take_s(k)
         if i == 0:
             load_in.wait()
         up(k)
-        if i + 1 < len(ORDER):
-            take_z(ORDER[i + 1])
-        if i:
-            fold_sib(ORDER[i - 1])
-        else:
+        if i == 0:
             load_dn.wait()
         down(k)
-        start(sib_copy(k))
         if i:
             fold_x(ORDER[i - 1])
+        start(sib_copy(k))
     fold_sib(ORDER[-1])
     fold_x(ORDER[-1])
     for k in range(1, 4):
@@ -268,7 +268,7 @@
             dma((4,)), dma((4,)), dma((4,)), dma((4,)), dma((4,)), dma((4,)),
         ],
         compiler_params=pltpu.CompilerParams(
-            collective_id=0, has_side_effects=True, vmem_limit_bytes=48 * 1024 * 1024),
+            collective_id=0, has_side_effects=True, vmem_limit_bytes=60 * 1024 * 1024),
         cost_estimate=pl.CostEstimate(
             flops=6 * hosts * rows * width * hidden, bytes_accessed=6 * width * hidden, transcendentals=0),
     )(tokens, expert_ids, gate_scores, host_expert, w_in[0], w_down[0])

time: 89.6 us -> 77.3 us (0.86)
  Pallas kernels: 83.6 us -> 72.6 us
  local copies, waits for them, and re-layouts: 5.74 us -> 4.42 us
    pallas_call x1, Pallas kernels: 83.6 us -> 72.6 us  [gathered_shards(): pl.pallas_call(fused_kernel, out_shape=jax.ShapeDtypeStruct((rows, width)...]
    unnamed x9 -> x3, local copies, waits for them, and re-layouts: 5.74 us -> 4.42 us
where the time goes in v2:
time: 77.3 us; the launch traced here: 77.1 us
  Pallas kernels  72.6 us (94%)
  local copies, waits for them, and re-layouts  4.42 us (6%)
    pallas_call x1, Pallas kernels, gathered_shards(): pl.pallas_call(fused_kernel, out_shape=jax.ShapeDtypeStruct((rows, width)...  72.6 us
    unnamed x3, local copies, waits for them, and re-layouts  4.42 us

profile of v2, /device:TPU:0, one launch (start us, length us, event | category | flops | bytes accessed | tf_op | source)
XLA Modules:
  0.0 77.1 jit_solution(8126982253855447420)
XLA Ops:
  0.0 1.4 %copy.7.ids_ref = s32[64,8]{1,0:T(8,128)} copy(s32[64,8]{0,1:T(8,128)} %param.7) | data formatting | bytes 4096 | tf_op args[1]
  1.4 1.4 %copy.8.gate_ref = f32[64,8]{1,0:T(8,128)} copy(f32[64,8]{0,1:T(8,128)} %param.8) | data formatting | bytes 4096 | tf_op args[2]
  2.8 72.6 %shard_map.64 = bf16[64,2048]{1,0:T(8,128)(2,1)} custom-call(bf16[64,2048]{1,0:T(8,128)(2,1)} %tok_ref.1, s32[64,8]{1,0:T(8,128)} %copy.7.ids_ref, f32[64,8]{1,0:T(8,128)} %copy.8.gate_ref, s32[16]{0:T(128)} %host_ref.1, bf16[2048,1536]{1,0:T(8,128)(2,1)} %bitcast.2, bf16[768,2048]{1,0:T(8,128)(2,1)} %bitcast.3), custom_call_target="tpu_custom_call" | custom-call | flops 9663676416 | bytes 9437184 | tf_op jit(solution)/shard_map/pallas_call | solution.py:248
  75.4 1.7 %copy.10 = bf16[64,2048]{1,0:T(8,128)(2,1)} copy(bf16[64,2048]{1,0:T(8,128)(2,1)} %shard_map.64) | data formatting | bytes 524288

commit v3 on v2

--- a/solution.py
+++ b/solution.py
@@ -68,7 +68,7 @@
 ):
     rows, width = tok_ref.shape
     experts = host_ref.shape[0]
-    top = ids_ref.shape[1]
+    top = ids_ref.shape[0]
     hidden = wdn_ref.shape[0]
     group = 4 * rows
     me = lax.axis_index("expert")
@@ -98,9 +98,9 @@
     held = jnp.full((rows, SIDE), -1, jnp.int32)
     for h in range(experts):
         held = jnp.where((lane == h) | (lane == h + experts), host_ref[h], held)
-    gate = gate_ref[...]
+    gate = gate_ref[...].T
     weights = gate / jnp.sum(gate, axis=1, keepdims=True)
-    ids = ids_ref[...]
+    ids = ids_ref[...].T
     dense = jnp.zeros((rows, SIDE), jnp.float32)
     for k in range(top):
         dense = dense + jnp.where(ids[:, k:k + 1] == held, weights[:, k:k + 1], 0.0)
@@ -271,7 +271,7 @@
             collective_id=0, has_side_effects=True, vmem_limit_bytes=60 * 1024 * 1024),
         cost_estimate=pl.CostEstimate(
             flops=6 * hosts * rows * width * hidden, bytes_accessed=6 * width * hidden, transcendentals=0),
-    )(tokens, expert_ids, gate_scores, host_expert, w_in[0], w_down[0])
+    )(tokens, expert_ids.T, gate_scores.T, host_expert, w_in[0], w_down[0])
 
 
 def solution(mesh):

time: 77.3 us -> 74.5 us (0.964)
  local copies, waits for them, and re-layouts: 4.42 us -> 1.67 us
    unnamed x3 -> x1, local copies, waits for them, and re-layouts: 4.42 us -> 1.67 us
where the time goes in v3:
time: 74.5 us; the launch traced here: 74.3 us
  Pallas kernels  72.6 us (97%)
  local copies, waits for them, and re-layouts  1.67 us (2%)
    pallas_call x1, Pallas kernels, gathered_shards(): pl.pallas_call(fused_kernel, out_shape=jax.ShapeDtypeStruct((rows, width)...  72.6 us
    unnamed x1, local copies, waits for them, and re-layouts  1.67 us

profile of v3, /device:TPU:0, one launch (start us, length us, event | category | flops | bytes accessed | tf_op | source)
XLA Modules:
  0.0 74.3 jit_solution(13126659543453981106)
XLA Ops:
  0.0 72.6 %shard_map.64 = bf16[64,2048]{1,0:T(8,128)(2,1)} custom-call(bf16[64,2048]{1,0:T(8,128)(2,1)} %tok_ref.1, s32[8,64]{1,0:T(8,128)} %bitcast.6, f32[8,64]{1,0:T(8,128)} %bitcast.7, s32[16]{0:T(128)} %host_ref.1, bf16[2048,1536]{1,0:T(8,128)(2,1)} %bitcast.4, bf16[768,2048]{1,0:T(8,128)(2,1)} %bitcast.5), custom_call_target="tpu_custom_call" | custom-call | flops 9663676416 | bytes 9437184 | tf_op jit(solution)/shard_map/pallas_call | solution.py:248
  72.7 1.7 %copy.8 = bf16[64,2048]{1,0:T(8,128)(2,1)} copy(bf16[64,2048]{1,0:T(8,128)(2,1)} %shard_map.64) | data formatting | bytes 524288
